TPU v7x, 32 devices: a whole 2x2x4 slice. The times are simulated.
32 devices in a mesh: parts: 2 (over y), dp: 4 (over z), tp: 4 (over x, core).
Axes of the slice: x: 2, y: 2, z: 4, core: 2. Of those that a mesh axis runs over, the one named last changes fastest.
Arguments:
- memory_hidden: bfloat16 [512, 5120], P(('parts', 'dp'), 'tp'), parts along dimension 0, may hold values from -6 to 6
- kv_weight: bfloat16 [2, 5120, 1024], P(None, None, 'tp'), may hold values from -0.078125 to 0.078125
- kv_bias: bfloat16 [2, 1024], P(None, 'tp'), may hold values from -3 to 3
- memory_sections: int32 [512], P('parts'), parts along dimension 0, may hold values from 0 to 3, never falling along the last dimension, each value on 1 to 128 neighbouring positions
- group_sections: int32 [8], P(('parts', 'dp')), parts along dimension 0, may hold values from 0 to 3
- queries: bfloat16 [64, 5120], P(('parts', 'dp'), 'tp'), parts along dimension 0, may hold values from -130 to 130
- new_keys: bfloat16 [64, 1024], P(('parts', 'dp'), 'tp'), parts along dimension 0, may hold values from -5 to 5
- new_values: bfloat16 [64, 1024], P(('parts', 'dp'), 'tp'), parts along dimension 0, may hold values from -5 to 5
- cache_keys: bfloat16 [32, 512, 1024], P(('parts', 'dp'), None, 'tp'), parts along dimension 0, may hold values from -5 to 5
- cache_values: bfloat16 [32, 512, 1024], P(('parts', 'dp'), None, 'tp'), parts along dimension 0, may hold values from -5 to 5
- cache_lengths: int32 [32], P(('parts', 'dp')), parts along dimension 0, may hold values from 2 to 512, as said below
- out_weight: bfloat16 [5120, 5120], P('tp', 'dp'), may hold values from -1.25 to 1.25
Outputs:
- output: bfloat16 [64, 5120], P(('parts', 'tp'), 'dp'), parts along dimension 0
There are 2 independent parts, one for each index of `parts`. A program takes and returns all parts, laid end to end along the dimension named above; an argument that names none is the same for every part. Nothing has to cross between parts.
Inputs may be any that keep to these rules, and one draw needn't show every extreme that they name: `memory_sections`: memory rows are grouped by section in order; every section holds at least one row. `cache_lengths`: some request has all 512 slots live.
All inputs are finite; a program needn't handle non-finite values.
Results may differ from a plain program's by a relative error of at most 0.0054.
Values may be sent and summed in bfloat16 or wider, within the bound.
A program may use at most 64 MiB of HBM per device.

v0:
```python
import jax
import jax.numpy as jnp
from jax import lax
from jax.sharding import PartitionSpec as P

D = 5120
HQ = 40
KVH = 8
HD = 128
MROWS = 256
NEW = 2
LMAX = 512


masked_score = -1e30


def body(
    memory_hidden,
    kv_weight,
    kv_bias,
    memory_sections,
    group_sections,
    queries,
    new_keys,
    new_values,
    cache_keys,
    cache_values,
    cache_lengths,
    out_weight,
):
    kv_cols = kv_weight.shape[2]
    piece = lax.all_gather(memory_hidden, "tp", axis=1, tiled=True)
    acc = jnp.einsum("md,sdc->smc", piece, kv_weight, preferred_element_type=jnp.float32)
    widened = piece.astype(jnp.float32)
    acc_kv = acc
    squares = jnp.sum(widened * widened, axis=1)
    scale = lax.rsqrt(squares / D + 1e-06)
    memory_kv = (acc_kv * scale[None, :, None] + kv_bias.astype(jnp.float32)[:, None, :]).astype(
        jnp.bfloat16
    )
    memory_all = lax.all_gather(memory_kv, "dp", axis=1, tiled=True)
    heads_kv = kv_cols // HD
    per_head = HQ // KVH
    requests = cache_lengths.shape[0]
    inv = 1.0 / HD**0.5
    query = queries.reshape(requests, NEW, heads_kv, per_head, HD)
    mem_keys = memory_all[0].reshape(MROWS, heads_kv, HD)
    mem_values = memory_all[1].reshape(MROWS, heads_kv, HD)
    fresh_keys = new_keys.reshape(requests, NEW, heads_kv, HD)
    fresh_values = new_values.reshape(requests, NEW, heads_kv, HD)
    old_keys = cache_keys.reshape(requests, LMAX, heads_kv, HD)
    old_values = cache_values.reshape(requests, LMAX, heads_kv, HD)
    mem_ok = (memory_sections == group_sections[0])[None, None, None, None, :]
    new_ok = (jnp.arange(NEW)[None, :] <= jnp.arange(NEW)[:, None])[None, :, None, None, :]
    s_mem = jnp.where(
        mem_ok,
        jnp.einsum("rnkgd,mkd->rnkgm", query, mem_keys, preferred_element_type=jnp.float32) * inv,
        masked_score,
    )
    s_new = jnp.where(
        new_ok,
        jnp.einsum("rnkgd,rjkd->rnkgj", query, fresh_keys, preferred_element_type=jnp.float32)
        * inv,
        masked_score,
    )
    top = jnp.maximum(jnp.max(s_mem, axis=-1), jnp.max(s_new, axis=-1))
    cache_ok = (jnp.arange(LMAX)[None, :] < cache_lengths[:, None])[:, None, None, None, :]
    s_cache = jnp.where(
        cache_ok,
        jnp.einsum("rnkgd,rlkd->rnkgl", query, old_keys, preferred_element_type=jnp.float32) * inv,
        masked_score,
    )
    top = jnp.maximum(top, jnp.max(s_cache, axis=-1))
    p_cache = jnp.where(cache_ok, jnp.exp(s_cache - top[..., None]), 0.0)
    p_cache_total = jnp.sum(p_cache, axis=-1)
    acc = jnp.einsum(
        "rnkgl,rlkd->rnkgd",
        p_cache.astype(jnp.bfloat16),
        old_values,
        preferred_element_type=jnp.float32,
    )
    p_mem = jnp.where(mem_ok, jnp.exp(s_mem - top[..., None]), 0.0)
    p_new = jnp.where(new_ok, jnp.exp(s_new - top[..., None]), 0.0)
    total = p_cache_total + jnp.sum(p_mem, axis=-1) + jnp.sum(p_new, axis=-1)
    acc = acc + jnp.einsum(
        "rnkgm,mkd->rnkgd",
        p_mem.astype(jnp.bfloat16),
        mem_values,
        preferred_element_type=jnp.float32,
    )
    acc = acc + jnp.einsum(
        "rnkgj,rjkd->rnkgd",
        p_new.astype(jnp.bfloat16),
        fresh_values,
        preferred_element_type=jnp.float32,
    )
    attended = (
        (acc / total[..., None])
        .astype(jnp.bfloat16)
        .reshape(requests * NEW, heads_kv * per_head * HD)
    )
    every_row = lax.all_gather(attended, "dp", axis=0, tiled=True)
    piece = every_row
    summed = lax.psum_scatter(
        jnp.dot(piece, out_weight, preferred_element_type=jnp.float32),
        "tp",
        scatter_dimension=0,
        tiled=True,
    )
    return summed.astype(jnp.bfloat16)


def solution(mesh):
    return jax.shard_map(
        body,
        mesh=mesh,
        in_specs=(
            P(("parts", "dp"), "tp"),
            P(None, None, "tp"),
            P(None, "tp"),
            P("parts"),
            P(("parts", "dp")),
            P(("parts", "dp"), "tp"),
            P(("parts", "dp"), "tp"),
            P(("parts", "dp"), "tp"),
            P(("parts", "dp"), None, "tp"),
            P(("parts", "dp"), None, "tp"),
            P(("parts", "dp")),
            P("tp", "dp"),
        ),
        out_specs=P(("parts", "tp"), "dp"),
        check_vma=False,
    )
```

profile of v0, /device:TPU:0, one launch (start us, length us, event | category | flops | bytes accessed | tf_op | source)
XLA Modules:
  0.0 102.7 jit_solution(17801640505676995683)
XLA Ops:
  6.5 0.0 copy-start
  6.5 0.0 reduce-scatter.2.cloned.1.call-start
  6.5 0.5 iota_compare_fusion.1
  7.1 9.7 %all_gather.9 = bf16[64,5120]{1,0:T(8,128)(2,1)S(1)} all-gather(bf16[64,1280]{1,0:T(8,128)(2,1)} %param.12), channel_id=1, replica_groups=mesh['parts'=2,'dp'=4,'tp'=4] {'tp'}, dimensions={1}, use_global_device_ids=true | all-gather | bytes 819200 | tf_op jit(solution)/shard_map/all_gather | solution.py:33
  16.7 0.2 multiply_reduce_fusion
  17.0 0.7 convert_element_type.28
  17.7 0.0 copy-start.3
  17.7 3.5 %fusion.6 = bf16[2,64,256]{2,1,0:T(8,128)(2,1)S(1)} fusion(bf16[2,5120,256]{2,1,0:T(8,128)(2,1)} %param.13, bf16[64,5120]{1,0:T(8,128)(2,1)S(1)} %all_gather.9, f32[2,256]{1,0:T(2,128)S(1)} %convert_element_type.28, f32[64]{0:T(128)S(1)} %add_rsqrt_fusion), kind=kOutput, calls=%fused_computation.10 | convolution fusion | flops 335642624 | bytes 5966080 | tf_op jit(solution)/shard_map/md,sdc->smc/dot_general | solution.py:34
  21.2 14.1 %all_gather.10 = bf16[2,256,256]{2,1,0:T(8,128)(2,1)S(1)} all-gather(bf16[2,64,256]{2,1,0:T(8,128)(2,1)S(1)} %fusion.6), channel_id=1, replica_groups=mesh['parts'=2,'dp'=4,'tp'=4] {'dp'}, dimensions={1}, use_global_device_ids=true | all-gather | bytes 327680 | tf_op jit(solution)/shard_map/all_gather | solution.py:42
  35.3 0.7 reshape_squeeze.6
  36.0 0.8 reshape.71
  37.4 0.0 copy-done.3
  37.5 0.0 copy-start.2
  37.5 1.2 %fusion.38 = (f32[4,2,2,5]{0,3,2,1:T(8,128)S(1)}, f32[4,2,2,5,256]{4,0,3,2,1:T(4,128)S(1)}) fusion(bf16[4,2,2,5,128]{4,3,2,1,0:T(8,128)(2,1)S(1)} %reshape.71, bf16[256,2,128,1,1]{2,1,0,4,3:T(2,128)(2,1)} %bitcast.41, pred[256]{0:T(512)(128)(4,1)S(1)} %broadcast_compare_fusion), kind=kOutput, calls=%fused_computation.55 | convolution fusion | flops 5304240 | bytes 234048 | tf_op jit(solution)/shard_map/rnkgd,mkd->rnkgm/dot_general | solution.py:58
  38.6 0.0 copy-done.2
  38.7 0.1 copy.74
  38.8 0.7 iota_compare_fusion
  39.5 0.0 copy-start.1
  39.5 2.2 %reshape.70 = bf16[4,512,2,128]{3,2,1,0:T(2,128)(2,1)} reshape(bf16[4,512,256]{2,1,0:T(8,128)(2,1)} %param.20) | data formatting | bytes 2097152 | tf_op jit(solution)/shard_map/reshape | solution.py:52
  41.7 0.7 reshape.72
  42.3 2.3 %fusion.37 = (f32[4,2,2,5]{3,1,2,0:T(2,128)S(1)}, f32[4,2,2,5,512]{4,3,1,2,0:T(8,128)}) fusion(bf16[4,2,2,5,128]{4,3,2,1,0:T(8,128)(2,1)S(1)} %reshape.71, bf16[4,512,2,128,1]{3,2,1,0,4:T(2,128)(2,1)} %bitcast.38, pred[4,512]{1,0:T(4,128)(4,1)S(1)} %iota_compare_fusion), kind=kOutput, calls=%fused_computation.54 | convolution fusion | flops 10608560 | bytes 1235264 | tf_op jit(solution)/shard_map/rnkgd,rlkd->rnkgl/dot_general | solution.py:71
  44.7 1.5 %fusion.39 = (f32[4,2,2,5]{3,1,2,0:T(2,128)S(1)}, f32[4,2,2,5,2]{3,4,1,2,0:T(2,128)}) fusion(bf16[4,2,2,5,128]{4,3,2,1,0:T(8,128)(2,1)S(1)} %reshape.71, bf16[4,2,2,128,1]{3,2,1,0,4:T(2,128)(2,1)S(1)} %bitcast.43, pred[2,2]{1,0:T(4,128)(4,1)} %iota_compare_fusion.1), kind=kOutput, calls=%fused_computation.56 | convolution fusion | flops 41360 | bytes 25540 | tf_op jit(solution)/shard_map/rnkgd,rjkd->rnkgj/dot_general | solution.py:63
  46.2 0.0 copy-done.1
  46.2 0.1 copy.79
  46.3 1.2 %fusion.16 = f32[4,2,2,5]{3,1,2,0:T(2,128)S(1)} fusion(f32[4,2,2,5,512]{4,3,1,2,0:T(8,128)} %get-tuple-element.10, f32[4,2,2,5]{3,1,2,0:T(2,128)S(1)} %copy.77, pred[4,512]{1,0:T(4,128)(4,1)} %copy-done.1), kind=kLoop, calls=%fused_computation.25 | loop fusion | flops 122800 | bytes 166528 | tf_op jit(solution)/shard_map/reduce_sum | solution.py:76
  47.5 1.4 %fusion.33 = f32[4,2,2,5]{3,1,2,0:T(2,128)} fusion(f32[4,2,2,5,2]{3,4,1,2,0:T(2,128)} %get-tuple-element.14, f32[4,2,2,5]{3,1,2,0:T(2,128)S(1)} %copy.77, pred[2,2]{1,0:T(4,128)(4,1)} %iota_compare_fusion.1), kind=kLoop, calls=%fused_computation.50 | loop fusion | flops 400 | bytes 1284 | tf_op jit(solution)/shard_map/reduce_sum | solution.py:85
  48.9 1.3 %fusion.25 = (f32[4,2,2,5]{0,3,2,1:T(8,128)S(1)}, bf16[4,2,2,5,256]{4,0,3,2,1:T(4,128)(2,1)}) fusion(f32[4,2,2,5,256]{4,0,3,2,1:T(4,128)S(1)} %get-tuple-element.12, f32[4,2,2,5]{0,3,2,1:T(8,128)S(1)} %copy.79, pred[256]{0:T(512)(128)(4,1)} %copy-done.2), kind=kLoop, calls=%fused_computation.34 | loop fusion | flops 81840 | bytes 123776 | tf_op jit(solution)/shard_map/reduce_sum | solution.py:85
  50.2 0.7 copy.85
  50.9 2.2 %reshape.73 = bf16[4,512,2,128]{3,2,1,0:T(2,128)(2,1)} reshape(bf16[4,512,256]{2,1,0:T(8,128)(2,1)} %param.21) | data formatting | bytes 2097152 | tf_op jit(solution)/shard_map/reshape | solution.py:53
  53.1 2.3 %convolution_bitcast_fusion.2 = f32[4,2,2,5,128]{4,3,1,2,0:T(8,128)} fusion(bf16[4,512,2,128,1]{3,2,1,0,4:T(2,128)(2,1)} %bitcast.39, f32[4,2,2,5,512]{4,3,1,2,0:T(8,128)} %get-tuple-element.10, f32[4,2,2,5]{3,1,2,0:T(2,128)S(1)} %copy.77, pred[4,512]{1,0:T(4,128)(4,1)} %copy-done.1), kind=kOutput, calls=%fused_computation.16 | convolution fusion | flops 10608640 | bytes 1255744 | tf_op jit(solution)/shard_map/rnkgl,rlkd->rnkgd/dot_general | solution.py:77
  55.4 0.7 reshape.74
  56.1 0.7 add_add_fusion
  56.8 1.0 fusion.9
  57.8 1.0 fusion.10
  58.9 13.5 %all_gather.11 = bf16[32,1280]{1,0:T(8,128)(2,1)S(1)} all-gather(bf16[8,1280]{1,0:T(8,128)(2,1)S(1)} %reshape.75), channel_id=1, replica_groups=mesh['parts'=2,'dp'=4,'tp'=4] {'dp'}, dimensions={0}, use_global_device_ids=true | all-gather | bytes 102400 | tf_op jit(solution)/shard_map/all_gather | solution.py:103
  72.4 0.0 copy-done
  72.4 1.3 %fusion.40 = f32[32,1280]{1,0:T(8,128)} fusion(bf16[32,1280]{1,0:T(8,128)(2,1)S(1)} %all_gather.11, bf16[1280,1280]{1,0:T(8,128)(2,1)S(1)} %copy-done), kind=kOutput, calls=%fused_computation.57 | convolution fusion | flops 104857600 | bytes 3522560 | tf_op jit(solution)/shard_map/dot_general | solution.py:106
  73.7 0.0 reduce-scatter.2.cloned.1.call-update
  73.7 20.7 %reduce-scatter.2.cloned.1.call-done = f32[8,1280]{1,0:T(8,128)} async-done(((f32[32,1280]{1,0:T(8,128)}), f32[8,1280]{1,0:T(8,128)}) %reduce-scatter.2.cloned.1.call-update) | async-done | bytes 40976 | tf_op jit(solution)/shard_map/reduce_scatter | solution.py:105
  94.4 1.4 %convert_element_type.35 = bf16[8,1280]{1,0:T(8,128)(2,1)} convert(f32[8,1280]{1,0:T(8,128)} %reduce-scatter.2.cloned.1.call-done) | non-fusion elementwise | flops 10240 | bytes 61440 | tf_op jit(solution)/shard_map/convert_element_type | solution.py:111
  (8 shorter events, 0.1 us)
Async XLA Ops:
  6.5 65.8 %copy-start = (bf16[1280,1280]{1,0:T(8,128)(2,1)S(1)}, bf16[1280,1280]{1,0:T(8,128)(2,1)}, u32[]{:S(2)}) copy-start(bf16[1280,1280]{1,0:T(8,128)(2,1)} %param.23) | copy-start | bytes 9830404
  6.5 87.9 %reduce-scatter.2.cloned.1.call-start = ((), (), s32[]{:S(2)}) async-start(), calls=%async_computation.1 | async-start | bytes 204800 | tf_op jit(solution)/shard_map/reduce_scatter | solution.py:105
  17.7 19.8 %copy-start.3 = (s32[256]{0:T(256)S(1)}, s32[256]{0:T(256)}, u32[]{:S(2)}) copy-start(s32[256]{0:T(256)} %param.15) | copy-start | bytes 3076
  37.5 1.2 %copy-start.2 = (pred[256]{0:T(512)(128)(4,1)}, pred[256]{0:T(512)(128)(4,1)S(1)}, u32[]{:S(2)}) copy-start(pred[256]{0:T(512)(128)(4,1)S(1)} %broadcast_compare_fusion) | copy-start | bytes 772
  39.5 6.7 %copy-start.1 = (pred[4,512]{1,0:T(4,128)(4,1)}, pred[4,512]{1,0:T(4,128)(4,1)S(1)}, u32[]{:S(2)}) copy-start(pred[4,512]{1,0:T(4,128)(4,1)S(1)} %iota_compare_fusion) | copy-start | bytes 6148
Sparse Core Ops, SparseCore 0:
  73.9 20.5 reduce-scatter.1
where the time goes:
time: 103 us
  blocking collectives  37.3 us (36%)
  waiting for transfers between devices  20.7 us (20%)
  matrix products  14.1 us (14%)
  between operations  14.1 us (14%)
  other arithmetic  8.22 us (8%)
  local copies, waits for them, and re-layouts  8.19 us (8%)
    reduce_scatter x1, waiting for transfers between devices, body(): lax.psum_scatter(jnp.dot(piece, out_weight, preferred_element_type=jnp.fl...  20.7 us
    all_gather x1, blocking collectives, body(): memory_all = lax.all_gather(memory_kv, 'dp', axis=1, tiled=True)  14.1 us
    all_gather x1, blocking collectives, body(): every_row = lax.all_gather(attended, 'dp', axis=0, tiled=True)  13.5 us
    all_gather x1, blocking collectives, body(): piece = lax.all_gather(memory_hidden, 'tp', axis=1, tiled=True)  9.66 us
    dot_general x1, matrix products, body(): jnp.einsum('md,sdc->smc', piece, kv_weight, preferred_element_type=jnp.fl...  3.52 us
    reduce_sum x2, other arithmetic, body(): total = p_cache_total + jnp.sum(p_mem, axis=-1) + jnp.sum(p_new, axis=-1)  2.75 us
    dot_general x1, matrix products, body(): jnp.einsum('rnkgd,rlkd->rnkgl', query, old_keys, preferred_element_type=j...  2.34 us
    dot_general x1, matrix products, body(): jnp.einsum('rnkgl,rlkd->rnkgd', p_cache.astype(jnp.bfloat16), old_values,...  2.26 us
  transfers between devices with their start and end apart: 1, of which 1 were waited for; matrix products, arithmetic and copies ran while one was open for 0% of the time, Pallas kernels for 0%

commit v1 on v0

v1 whole, which is shorter than its diff:
```python
import functools

import jax
import jax.numpy as jnp
from jax import lax
from jax.experimental import pallas as pl
from jax.experimental.pallas import tpu as pltpu
from jax.sharding import PartitionSpec as P

D = 5120
HQ = 40
KVH = 8
HD = 128
NEW = 2
LMAX = 512
PER = HQ // KVH
INV = 1.0 / HD**0.5
MASKED = -1e30
MESH = pl.DeviceIdType.MESH
F32 = jnp.float32
BF16 = jnp.bfloat16


def up(n, m):
    return -(-n // m) * m


def nt(a, b):
    return lax.dot_general(a, b, (((1,), (1,)), ((), ())), preferred_element_type=F32)


def tn(a, b):
    return lax.dot_general(a, b, (((0,), (0,)), ((), ())), preferred_element_type=F32)


def nn(a, b):
    return lax.dot_general(a, b, (((1,), (0,)), ((), ())), preferred_element_type=F32)


def kernel(
    tp,
    dp,
    lens,
    group,
    hidden_h,
    kvw_h,
    bias_h,
    sections_h,
    q_h,
    nk_h,
    nv_h,
    ck_h,
    cv_h,
    wo_h,
    out,
    hid,
    kvw,
    bias,
    sections,
    q_v,
    nk,
    nv,
    ck,
    cv,
    wo,
    qm,
    acc_s,
    acc_r,
    st_s,
    st_r,
    att,
    osum_s,
    osum_r,
    load_sem,
    hid_ss,
    hid_rs,
    q_ss,
    q_rs,
    acc_ss,
    acc_rs,
    st_ss,
    st_rs,
    att_ss,
    att_rs,
    o_ss,
    o_rs,
):
    t = lax.axis_index("tp")
    d = lax.axis_index("dp")
    mdev, feat = hid.shape[1], hid.shape[2]
    rows, heads = q_v.shape[0], kvw.shape[2] // HD
    requests = ck.shape[0]
    qr = PER * rows
    qp = qm.shape[2]

    def at_tp(off):
        return {"tp": lax.rem(t + off, tp)}

    def at_dp(off):
        return {"dp": lax.rem(d + off + dp, dp)}

    pairs = (
        (q_h, q_v),
        (hidden_h, hid.at[0]),
        (nk_h, nk),
        (nv_h, nv),
        (bias_h, bias),
        (sections_h, sections),
        (ck_h, ck),
        (cv_h, cv),
        (kvw_h, kvw),
        (wo_h, wo),
    )
    loads = [pltpu.make_async_copy(s, v, load_sem.at[i]) for i, (s, v) in enumerate(pairs)]
    for copy in loads:
        copy.start()
    l_q, l_hid, l_nk, l_nv, l_bias, l_sec, l_ck, l_cv, l_kvw, l_wo = loads

    barrier = pltpu.get_barrier_semaphore()
    for off in range(1, tp):
        pl.semaphore_signal(barrier, inc=1, device_id=at_tp(off), device_id_type=MESH)
    for off in range(1, dp):
        pl.semaphore_signal(barrier, inc=1, device_id=at_dp(off), device_id_type=MESH)

    l_q.wait()
    q_wide = q_v[...].astype(F32)
    section_rows = jnp.full((qp - qr, HD), group[0], F32)
    for k in range(heads):
        parts = [q_wide[:, (k * PER + g) * HD : (k * PER + g + 1) * HD] for g in range(PER)]
        qm[0, k] = jnp.concatenate(parts + [section_rows], axis=0).astype(BF16)
    st_s[...] = jnp.zeros_like(st_s)

    l_hid.wait()
    pl.semaphore_wait(barrier, tp - 1 + dp - 1)

    def send(src, dst, ss, rs, to):
        copy = pltpu.make_async_remote_copy(
            src_ref=src, dst_ref=dst, send_sem=ss, recv_sem=rs, device_id=to, device_id_type=MESH
        )
        copy.start()
        return copy

    hid_c = [None] * tp
    for off in range(1, tp):
        hid_c[off] = send(hid.at[0], hid.at[off], hid_ss.at[off], hid_rs.at[off], at_tp(off))
    q_c = [None] * dp
    for off in range(1, dp):
        q_c[off] = send(qm.at[0], qm.at[off], q_ss.at[off], q_rs.at[off], at_dp(off))

    for copy in (l_nk, l_nv, l_ck, l_cv, l_bias, l_sec):
        copy.wait()
    row = lax.broadcasted_iota(jnp.int32, (qr, 1), 0)
    token = lax.rem(row, rows)
    request = lax.div(token, NEW)
    slot = lax.broadcasted_iota(jnp.int32, (1, LMAX), 1)
    fresh = lax.broadcasted_iota(jnp.int32, (1, rows), 1)
    new_ok = (lax.div(fresh, NEW) == request) & (fresh <= token)
    own = []
    for k in range(heads):
        cols = slice(k * HD, (k + 1) * HD)
        qk = qm[0, k][:qr]
        scores = [jnp.where(new_ok, nt(qk, nk[:, cols]) * INV, MASKED)]
        for r in range(requests):
            ok = (request == r) & (slot < lens[r])
            scores.append(jnp.where(ok, nt(qk, ck[r, :, cols]) * INV, MASKED))
        top = functools.reduce(
            jnp.maximum, [jnp.max(s, axis=1, keepdims=True) for s in scores]
        )
        weights = [jnp.exp(s - top) for s in scores]
        total = functools.reduce(jnp.add, [jnp.sum(p, axis=1, keepdims=True) for p in weights])
        acc = nn(weights[0].astype(BF16), nv[:, cols])
        for r in range(requests):
            acc = acc + nn(weights[r + 1].astype(BF16), cv[r, :, cols])
        own.append((top, total, acc))

    l_kvw.wait()
    proj = [jnp.zeros((mdev, heads * HD), F32) for _ in range(2)]
    squares = jnp.zeros((mdev, 1), F32)
    for off in range(tp):
        if off:
            hid_c[off].wait_recv()
        piece = hid[off]
        wide = piece.astype(F32)
        squares = squares + jnp.sum(wide * wide, axis=1, keepdims=True)
        first = pl.multiple_of(lax.rem(t - off + tp, tp) * feat, feat)
        for s in range(2):
            proj[s] = proj[s] + nn(piece, kvw[s, pl.ds(first, feat), :])
    scale = lax.rsqrt(squares / D + 1e-06)
    mem_k, mem_v = [
        (proj[s] * scale + bias[s : s + 1, :].astype(F32)).astype(BF16) for s in range(2)
    ]

    mrows = sections.shape[1]
    lane = lax.broadcasted_iota(jnp.int32, (mdev, mrows), 1)
    place = lax.broadcasted_iota(jnp.int32, (mdev, mrows), 0) + d * mdev
    mine = jnp.where(lane == place, sections[...].astype(F32), 0.0)
    section = jnp.sum(mine, axis=1, keepdims=True)
    acc_c = [None] * dp
    st_c = [None] * dp
    for off in list(range(1, dp)) + [0]:
        if off:
            q_c[off].wait_recv()
        for k in range(heads):
            cols = slice(k * HD, (k + 1) * HD)
            qk = qm[off, k]
            ok = section == qk[qr : qr + 1, 0:1].astype(F32)
            s = jnp.where(ok, nt(mem_k[:, cols], qk) * INV, MASKED)
            top = jnp.max(s, axis=0, keepdims=True)
            p = jnp.where(ok, jnp.exp(s - top), 0.0)
            acc_s[off, k] = tn(p.astype(BF16), mem_v[:, cols]).astype(BF16)
            st_s[off, 2 * k : 2 * k + 1, 0:qp] = top
            st_s[off, 2 * k + 1 : 2 * k + 2, 0:qp] = jnp.sum(p, axis=0, keepdims=True)
        if off:
            st_c[off] = send(st_s.at[off], st_r.at[off], st_ss.at[off], st_rs.at[off], at_dp(-off))
            acc_c[off] = send(
                acc_s.at[off], acc_r.at[off], acc_ss.at[off], acc_rs.at[off], at_dp(-off)
            )

    for off in range(1, dp):
        st_c[off].wait_recv()
        acc_c[off].wait_recv()
    stats = [jnp.transpose((st_r if off else st_s)[off]) for off in range(dp)]
    blocks = []
    for k in range(heads):
        top_c, total_c, acc = own[k]
        tops = [st[:qr, 2 * k : 2 * k + 1] for st in stats]
        totals = [st[:qr, 2 * k + 1 : 2 * k + 2] for st in stats]
        top = functools.reduce(jnp.maximum, tops, top_c)
        factor = jnp.exp(top_c - top)
        total = total_c * factor
        acc = acc * factor
        for off in range(dp):
            factor = jnp.exp(tops[off] - top)
            total = total + totals[off] * factor
            acc = acc + (acc_r if off else acc_s)[off, k][:qr].astype(F32) * factor
        blocks.append(acc / total)
    ar = att.shape[1]
    if ar > heads * qr:
        blocks.append(jnp.zeros((ar - heads * qr, HD), F32))
    att[0] = jnp.concatenate(blocks, axis=0).astype(BF16)
    att_c = [None] * dp
    for off in range(1, dp):
        att_c[off] = send(att.at[0], att.at[off], att_ss.at[off], att_rs.at[off], at_dp(off))

    l_wo.wait()
    for off in range(1, dp):
        att_c[off].wait_recv()
    groups = []
    for g in range(dp):
        a = att[lax.rem(d - g + dp, dp)].astype(F32)
        groups.append(
            jnp.concatenate([a[h * rows : (h + 1) * rows] for h in range(heads * PER)], axis=1)
        )
    lhs = jnp.concatenate(groups, axis=0).astype(BF16)
    orows = osum_s.shape[1]
    result = nn(lhs, wo[...])
    for i in range(tp):
        osum_s[i] = result[i * orows : (i + 1) * orows]
    o_c = [None] * tp
    for off in range(1, tp):
        to = lax.rem(t + off, tp)
        o_c[off] = send(osum_s.at[to], osum_r.at[off], o_ss.at[off], o_rs.at[off], at_tp(off))
    summed = osum_s[t]
    for off in range(1, tp):
        o_c[off].wait_recv()
        summed = summed + osum_r[off]
    out[...] = summed.astype(BF16)

    for copies in (hid_c, q_c, st_c, acc_c, att_c, o_c):
        for copy in copies:
            if copy is not None:
                copy.wait_send()


def body(
    tp,
    dp,
    memory_hidden,
    kv_weight,
    kv_bias,
    memory_sections,
    group_sections,
    queries,
    new_keys,
    new_values,
    cache_keys,
    cache_values,
    cache_lengths,
    out_weight,
):
    mdev, feat = memory_hidden.shape
    heads = kv_weight.shape[2] // HD
    rows = queries.shape[0]
    qp = up(PER * rows + 1, 16)
    ar = up(heads * PER * rows, 16)
    ocols = out_weight.shape[1]
    orows = dp * rows // tp
    any_spec = pl.BlockSpec(memory_space=pl.ANY)
    smem = pl.BlockSpec(memory_space=pltpu.SMEM)
    dma = pltpu.SemaphoreType.DMA
    like = lambda a: pltpu.VMEM(a.shape, a.dtype)
    sections = memory_sections.reshape(1, -1)
    return pl.pallas_call(
        functools.partial(kernel, tp, dp),
        out_shape=jax.ShapeDtypeStruct((orows, ocols), BF16),
        in_specs=[smem, smem] + [any_spec] * 10,
        out_specs=pl.BlockSpec(memory_space=pltpu.VMEM),
        scratch_shapes=[
            pltpu.VMEM((tp, mdev, feat), BF16),
            like(kv_weight),
            like(kv_bias),
            like(sections),
            like(queries),
            like(new_keys),
            like(new_values),
            like(cache_keys),
            like(cache_values),
            like(out_weight),
            pltpu.VMEM((dp, heads, qp, HD), BF16),
            pltpu.VMEM((dp, heads, qp, HD), BF16),
            pltpu.VMEM((dp, heads, qp, HD), BF16),
            pltpu.VMEM((dp, 8, HD), F32),
            pltpu.VMEM((dp, 8, HD), F32),
            pltpu.VMEM((dp, ar, HD), BF16),
            pltpu.VMEM((tp, orows, ocols), F32),
            pltpu.VMEM((tp, orows, ocols), F32),
            dma((10,)),
            dma((tp,)),
            dma((tp,)),
        ]
        + [dma((dp,))] * 8
        + [dma((tp,))] * 2,
        compiler_params=pltpu.CompilerParams(
            collective_id=0, has_side_effects=True, vmem_limit_bytes=48 * 1024 * 1024
        ),
        name="decode_step",
    )(
        cache_lengths,
        group_sections,
        memory_hidden,
        kv_weight,
        kv_bias,
        sections,
        queries,
        new_keys,
        new_values,
        cache_keys,
        cache_values,
        out_weight,
    )


def solution(mesh):
    return jax.shard_map(
        functools.partial(body, mesh.shape["tp"], mesh.shape["dp"]),
        mesh=mesh,
        in_specs=(
            P(("parts", "dp"), "tp"),
            P(None, None, "tp"),
            P(None, "tp"),
            P("parts"),
            P(("parts", "dp")),
            P(("parts", "dp"), "tp"),
            P(("parts", "dp"), "tp"),
            P(("parts", "dp"), "tp"),
            P(("parts", "dp"), None, "tp"),
            P(("parts", "dp"), None, "tp"),
            P(("parts", "dp")),
            P("tp", "dp"),
        ),
        out_specs=P(("parts", "tp"), "dp"),
        check_vma=False,
    )
```

time: 103 us -> 37.2 us (0.36)
  blocking collectives: 37.3 us -> 0 us
  Pallas kernels: 0 us -> 26.1 us
  waiting for transfers between devices: 20.7 us -> 0 us
  matrix products: 14.1 us -> 0 us
  between operations: 14.1 us -> 0.68 us
  other arithmetic: 8.22 us -> 0 us
  local copies, waits for them, and re-layouts: 8.19 us -> 10 us
    all_gather x3 -> x0, blocking collectives: 37.3 us -> none  [the longest x1 14.1 us: body(): memory_all = lax.all_gather(memory_kv, 'dp', axis=1, tiled=True)]
    pallas_call x0 -> x1, Pallas kernels: none -> 26.1 us  [body(): pl.pallas_call(functools.partial(kernel, tp, dp), out_shape=jax.ShapeDtyp...]
    reduce_scatter x1 -> x0, waiting for transfers between devices: 20.7 us -> none  [body(): lax.psum_scatter(jnp.dot(piece, out_weight, preferred_element_type=jnp.fl...]
    dot_general x8 -> x0, matrix products: 14.1 us -> none  [the longest x1 3.52 us: body(): jnp.einsum('md,sdc->smc', piece, kv_weight, preferred_element_type=jnp.fl...]
    unnamed x8 -> x21, local copies, waits for them, and re-layouts: 0.02 us -> 10 us
    reshape x6 -> x0, local copies, waits for them, and re-layouts: 6.52 us -> none  [the longest x1 2.16 us: body(): old_keys = cache_keys.reshape(requests, LMAX, heads_kv, HD)]
    reduce_sum x4 -> x0, other arithmetic: 4.14 us -> none  [the longest x2 2.75 us: body(): total = p_cache_total + jnp.sum(p_mem, axis=-1) + jnp.sum(p_new, axis=-1)]
    convert_element_type x2 -> x0, other arithmetic: 2.07 us -> none  [the longest x1 1.39 us: body(): return summed.astype(jnp.bfloat16)]
  transfers between devices with their start and end apart: 1 -> 0, of which waited for: 1 -> 0; matrix products, arithmetic and copies ran while one was open for 0% -> 0% of each run, Pallas kernels for 0% -> 0%
where the time goes in v1:
time: 37.2 us; the launch traced here: 36.7 us
  Pallas kernels  26.1 us (70%)
  local copies, waits for them, and re-layouts  10 us (27%)
  between operations  0.68 us (2%)
    pallas_call x1, Pallas kernels, body(): pl.pallas_call(functools.partial(kernel, tp, dp), out_shape=jax.ShapeDtyp...  26.1 us
    unnamed x21, local copies, waits for them, and re-layouts  10 us

profile of v1, /device:TPU:0, one launch (start us, length us, event | category | flops | bytes accessed | tf_op | source)
XLA Modules:
  0.0 36.7 jit_solution(15170996084042176959)
XLA Ops:
  0.7 0.0 copy-start
  0.7 1.9 %copy-done = bf16[1280,1280]{1,0:T(8,128)(2,1)S(1)} copy-done((bf16[1280,1280]{1,0:T(8,128)(2,1)S(1)}, bf16[1280,1280]{1,0:T(8,128)(2,1)}, u32[]{:S(2)}) %copy-start) | copy-done | bytes 3276824
  2.6 0.0 copy-start.1
  2.6 1.2 %copy-done.1 = bf16[4,512,256]{2,1,0:T(8,128)(2,1)S(1)} copy-done((bf16[4,512,256]{2,1,0:T(8,128)(2,1)S(1)}, bf16[4,512,256]{2,1,0:T(8,128)(2,1)}, u32[]{:S(2)}) %copy-start.1) | copy-done | bytes 1048600
  3.8 0.0 copy-start.2
  3.8 1.2 %copy-done.2 = bf16[4,512,256]{2,1,0:T(8,128)(2,1)S(1)} copy-done((bf16[4,512,256]{2,1,0:T(8,128)(2,1)S(1)}, bf16[4,512,256]{2,1,0:T(8,128)(2,1)}, u32[]{:S(2)}) %copy-start.2) | copy-done | bytes 1048600
  5.0 0.0 copy-start.3
  5.0 0.9 %copy-done.3 = bf16[64,1280]{1,0:T(8,128)(2,1)S(1)} copy-done((bf16[64,1280]{1,0:T(8,128)(2,1)S(1)}, bf16[64,1280]{1,0:T(8,128)(2,1)}, u32[]{:S(2)}) %copy-start.3) | copy-done | bytes 163864
  5.9 0.0 copy-start.4
  5.9 0.7 %copy-done.4 = bf16[8,1280]{1,0:T(8,128)(2,1)S(1)} copy-done((bf16[8,1280]{1,0:T(8,128)(2,1)S(1)}, bf16[8,1280]{1,0:T(8,128)(2,1)}, u32[]{:S(2)}) %copy-start.4) | copy-done | bytes 20504
  6.7 0.0 copy-start.5
  6.7 0.7 %copy-done.5 = bf16[8,256]{1,0:T(8,128)(2,1)S(1)} copy-done((bf16[8,256]{1,0:T(8,128)(2,1)S(1)}, bf16[8,256]{1,0:T(8,128)(2,1)}, u32[]{:S(2)}) %copy-start.5) | copy-done | bytes 4120
  7.4 0.0 copy-start.6
  7.4 0.7 %copy-done.6 = bf16[8,256]{1,0:T(8,128)(2,1)S(1)} copy-done((bf16[8,256]{1,0:T(8,128)(2,1)S(1)}, bf16[8,256]{1,0:T(8,128)(2,1)}, u32[]{:S(2)}) %copy-start.6) | copy-done | bytes 4120
  8.0 0.0 copy-start.7
  8.1 0.7 %copy-done.7 = bf16[2,256]{1,0:T(2,128)(2,1)S(1)} copy-done((bf16[2,256]{1,0:T(2,128)(2,1)S(1)}, bf16[2,256]{1,0:T(2,128)(2,1)}, u32[]{:S(2)}) %copy-start.7) | copy-done | bytes 1048
  8.7 0.0 copy-start.8
  8.7 0.7 %copy-done.8 = s32[256]{0:T(256)S(1)} copy-done((s32[256]{0:T(256)S(1)}, s32[256]{0:T(256)}, u32[]{:S(2)}) %copy-start.8) | copy-done | bytes 1048
  9.4 0.0 copy-start.9
  9.4 0.7 %copy-done.9 = s32[4]{0:T(128)S(1)} copy-done((s32[4]{0:T(128)S(1)}, s32[4]{0:T(128)}, u32[]{:S(2)}) %copy-start.9) | copy-done | bytes 40
  10.1 26.1 %decode_step.1 = bf16[8,1280]{1,0:T(8,128)(2,1)S(1)} custom-call(s32[4]{0:T(128)S(1)} %copy-done.9, s32[1]{0:T(128)S(6)} %copy.14.group, bf16[64,1280]{1,0:T(8,128)(2,1)S(1)} %copy-done.3, bf16[2,5120,256]{2,1,0:T(8,128)(2,1)} %kvw_h.1, bf16[2,256]{1,0:T(2,128)(2,1)S(1)} %copy-done.7, s32[1,256]{1,0:T(1,128)S(1)} %bitcast.1, bf16[8,1280]{1,0:T(8,128)(2,1)S(1)} %copy-done.4, ...), custom_call_target="tpu_custom_call" | custom-call | tf_op jit(solution)/shard_map/decode_step/pallas_call | solution.py:303
  36.1 0.6 %copy.15 = bf16[8,1280]{1,0:T(8,128)(2,1)} copy(bf16[8,1280]{1,0:T(8,128)(2,1)S(1)} %decode_step.1) | data formatting | bytes 40960
Async XLA Ops:
  0.7 1.9 %copy-start = (bf16[1280,1280]{1,0:T(8,128)(2,1)S(1)}, bf16[1280,1280]{1,0:T(8,128)(2,1)}, u32[]{:S(2)}) copy-start(bf16[1280,1280]{1,0:T(8,128)(2,1)} %wo_h.1) | copy-start | bytes 9830404
  2.6 1.2 %copy-start.1 = (bf16[4,512,256]{2,1,0:T(8,128)(2,1)S(1)}, bf16[4,512,256]{2,1,0:T(8,128)(2,1)}, u32[]{:S(2)}) copy-start(bf16[4,512,256]{2,1,0:T(8,128)(2,1)} %ck_h.1) | copy-start | bytes 3145732
  3.8 1.2 %copy-start.2 = (bf16[4,512,256]{2,1,0:T(8,128)(2,1)S(1)}, bf16[4,512,256]{2,1,0:T(8,128)(2,1)}, u32[]{:S(2)}) copy-start(bf16[4,512,256]{2,1,0:T(8,128)(2,1)} %cv_h.1) | copy-start | bytes 3145732
  5.0 0.9 %copy-start.3 = (bf16[64,1280]{1,0:T(8,128)(2,1)S(1)}, bf16[64,1280]{1,0:T(8,128)(2,1)}, u32[]{:S(2)}) copy-start(bf16[64,1280]{1,0:T(8,128)(2,1)} %hidden_h.1) | copy-start | bytes 491524
  5.9 0.7 %copy-start.4 = (bf16[8,1280]{1,0:T(8,128)(2,1)S(1)}, bf16[8,1280]{1,0:T(8,128)(2,1)}, u32[]{:S(2)}) copy-start(bf16[8,1280]{1,0:T(8,128)(2,1)} %q_h.1) | copy-start | bytes 61444
  6.7 0.7 %copy-start.5 = (bf16[8,256]{1,0:T(8,128)(2,1)S(1)}, bf16[8,256]{1,0:T(8,128)(2,1)}, u32[]{:S(2)}) copy-start(bf16[8,256]{1,0:T(8,128)(2,1)} %nk_h.1) | copy-start | bytes 12292
  7.4 0.7 %copy-start.6 = (bf16[8,256]{1,0:T(8,128)(2,1)S(1)}, bf16[8,256]{1,0:T(8,128)(2,1)}, u32[]{:S(2)}) copy-start(bf16[8,256]{1,0:T(8,128)(2,1)} %nv_h.1) | copy-start | bytes 12292
  8.0 0.7 %copy-start.7 = (bf16[2,256]{1,0:T(2,128)(2,1)S(1)}, bf16[2,256]{1,0:T(2,128)(2,1)}, u32[]{:S(2)}) copy-start(bf16[2,256]{1,0:T(2,128)(2,1)} %bias_h.1) | copy-start | bytes 3076
  8.7 0.7 %copy-start.8 = (s32[256]{0:T(256)S(1)}, s32[256]{0:T(256)}, u32[]{:S(2)}) copy-start(s32[256]{0:T(256)} %param.15) | copy-start | bytes 3076
  9.4 0.7 %copy-start.9 = (s32[4]{0:T(128)S(1)}, s32[4]{0:T(128)}, u32[]{:S(2)}) copy-start(s32[4]{0:T(128)} %lens.1) | copy-start | bytes 52

commit v2 on v1

--- a/solution.py
+++ b/solution.py
@@ -331,7 +331,7 @@
         + [dma((dp,))] * 8
         + [dma((tp,))] * 2,
         compiler_params=pltpu.CompilerParams(
-            collective_id=0, has_side_effects=True, vmem_limit_bytes=48 * 1024 * 1024
+            collective_id=0, has_side_effects=True, vmem_limit_bytes=63 * 1024 * 1024
         ),
         name="decode_step",
     )(

time: 37.2 us -> 28.2 us (0.76)
  local copies, waits for them, and re-layouts: 10 us -> 1.34 us
    unnamed x21 -> x1, local copies, waits for them, and re-layouts: 10 us -> 1.34 us
where the time goes in v2:
time: 28.2 us; the launch traced here: 28 us
  Pallas kernels  26 us (92%)
  local copies, waits for them, and re-layouts  1.34 us (5%)
  between operations  0.66 us (2%)
    pallas_call x1, Pallas kernels, body(): pl.pallas_call(functools.partial(kernel, tp, dp), out_shape=jax.ShapeDtyp...  26 us
    unnamed x1, local copies, waits for them, and re-layouts  1.34 us

profile of v2, /device:TPU:0, one launch (start us, length us, event | category | flops | bytes accessed | tf_op | source)
XLA Modules:
  0.0 28.0 jit_solution(6007745258768965131)
XLA Ops:
  0.7 26.0 %decode_step.1 = bf16[8,1280]{1,0:T(8,128)(2,1)} custom-call(s32[4]{0:T(128)} %lens.1, s32[1]{0:T(128)S(6)} %copy.14.group, bf16[64,1280]{1,0:T(8,128)(2,1)} %hidden_h.1, bf16[2,5120,256]{2,1,0:T(8,128)(2,1)} %kvw_h.1, bf16[2,256]{1,0:T(2,128)(2,1)} %bias_h.1, s32[1,256]{1,0:T(1,128)} %bitcast.1, bf16[8,1280]{1,0:T(8,128)(2,1)} %q_h.1, bf16[8,256]{1,0:T(8,128)(2,1)} %nk_h.1, ...), custom_call_target="tpu_custom_call" | custom-call | tf_op jit(solution)/shard_map/decode_step/pallas_call | solution.py:303
  26.7 1.3 %copy.15 = bf16[8,1280]{1,0:T(8,128)(2,1)} copy(bf16[8,1280]{1,0:T(8,128)(2,1)} %decode_step.1) | data formatting | bytes 40960

commit v3 on v2

--- a/solution.py
+++ b/solution.py
@@ -69,6 +69,7 @@
     st_s,
     st_r,
     att,
+    osum,
     osum_s,
     osum_r,
     load_sem,
@@ -87,7 +88,9 @@
 ):
     t = lax.axis_index("tp")
     d = lax.axis_index("dp")
-    mdev, feat = hid.shape[1], hid.shape[2]
+    chunks, mdev, width = hid.shape[1:]
+    feat = chunks * width
+    relay = tp == 4
     rows, heads = q_v.shape[0], kvw.shape[2] // HD
     requests = ck.shape[0]
     qr = PER * rows
@@ -101,7 +104,6 @@
 
     pairs = (
         (q_h, q_v),
-        (hidden_h, hid.at[0]),
         (nk_h, nk),
         (nv_h, nv),
         (bias_h, bias),
@@ -110,17 +112,50 @@
         (cv_h, cv),
         (kvw_h, kvw),
         (wo_h, wo),
+    ) + tuple(
+        (hidden_h.at[:, c * width : (c + 1) * width], hid.at[0, c]) for c in range(chunks)
     )
     loads = [pltpu.make_async_copy(s, v, load_sem.at[i]) for i, (s, v) in enumerate(pairs)]
     for copy in loads:
         copy.start()
-    l_q, l_hid, l_nk, l_nv, l_bias, l_sec, l_ck, l_cv, l_kvw, l_wo = loads
+    l_q, l_nk, l_nv, l_bias, l_sec, l_ck, l_cv, l_kvw, l_wo = loads[:9]
 
     barrier = pltpu.get_barrier_semaphore()
     for off in range(1, tp):
         pl.semaphore_signal(barrier, inc=1, device_id=at_tp(off), device_id_type=MESH)
     for off in range(1, dp):
         pl.semaphore_signal(barrier, inc=1, device_id=at_dp(off), device_id_type=MESH)
+
+    pl.semaphore_wait(barrier, tp - 1 + dp - 1)
+
+    def send(src, dst, ss, rs, to):
+        copy = pltpu.make_async_remote_copy(
+            src_ref=src, dst_ref=dst, send_sem=ss, recv_sem=rs, device_id=to, device_id_type=MESH
+        )
+        copy.start()
+        return copy
+
+    if relay:
+        source = [t, t + 1 - 2 * lax.rem(t, 2), lax.rem(t + 2, tp), tp - 1 - t]
+        direct = {2: source[2], 1: source[1]}
+    else:
+        source = [lax.rem(t - off + tp, tp) for off in range(tp)]
+        direct = {off: lax.rem(t + off, tp) for off in range(1, tp)}
+    hid_c = [[None] * chunks for _ in range(tp)]
+
+    def send_hidden(slot, c, src, to):
+        hid_c[slot][c] = send(
+            src, hid.at[slot, c], hid_ss.at[slot, c], hid_rs.at[slot, c], {"tp": to}
+        )
+
+    def hand_on(c):
+        if relay:
+            hid_c[2][c].wait_recv()
+            send_hidden(3, c, hid.at[2, c], source[1])
+
+    for slot, to in direct.items():
+        for c in range(chunks):
+            send_hidden(slot, c, hidden_h.at[:, c * width : (c + 1) * width], to)
 
     l_q.wait()
     q_wide = q_v[...].astype(F32)
@@ -130,19 +165,6 @@
         qm[0, k] = jnp.concatenate(parts + [section_rows], axis=0).astype(BF16)
     st_s[...] = jnp.zeros_like(st_s)
 
-    l_hid.wait()
-    pl.semaphore_wait(barrier, tp - 1 + dp - 1)
-
-    def send(src, dst, ss, rs, to):
-        copy = pltpu.make_async_remote_copy(
-            src_ref=src, dst_ref=dst, send_sem=ss, recv_sem=rs, device_id=to, device_id_type=MESH
-        )
-        copy.start()
-        return copy
-
-    hid_c = [None] * tp
-    for off in range(1, tp):
-        hid_c[off] = send(hid.at[0], hid.at[off], hid_ss.at[off], hid_rs.at[off], at_tp(off))
     q_c = [None] * dp
     for off in range(1, dp):
         q_c[off] = send(qm.at[0], qm.at[off], q_ss.at[off], q_rs.at[off], at_dp(off))
@@ -172,19 +194,28 @@
         for r in range(requests):
             acc = acc + nn(weights[r + 1].astype(BF16), cv[r, :, cols])
         own.append((top, total, acc))
+        if k < chunks:
+            hand_on(k)
 
     l_kvw.wait()
     proj = [jnp.zeros((mdev, heads * HD), F32) for _ in range(2)]
     squares = jnp.zeros((mdev, 1), F32)
-    for off in range(tp):
-        if off:
-            hid_c[off].wait_recv()
-        piece = hid[off]
-        wide = piece.astype(F32)
-        squares = squares + jnp.sum(wide * wide, axis=1, keepdims=True)
-        first = pl.multiple_of(lax.rem(t - off + tp, tp) * feat, feat)
-        for s in range(2):
-            proj[s] = proj[s] + nn(piece, kvw[s, pl.ds(first, feat), :])
+    for copy in loads[9:]:
+        copy.wait()
+    handed = min(heads, chunks)
+    for slot in range(tp):
+        if relay and slot == 2:
+            for c in range(handed, chunks):
+                hand_on(c)
+        for c in range(chunks):
+            if slot and not (relay and slot == 2):
+                hid_c[slot][c].wait_recv()
+            piece = hid[slot, c]
+            wide = piece.astype(F32)
+            squares = squares + jnp.sum(wide * wide, axis=1, keepdims=True)
+            first = pl.multiple_of(source[slot] * feat + c * width, width)
+            for s in range(2):
+                proj[s] = proj[s] + nn(piece, kvw[s, pl.ds(first, width), :])
     scale = lax.rsqrt(squares / D + 1e-06)
     mem_k, mem_v = [
         (proj[s] * scale + bias[s : s + 1, :].astype(F32)).astype(BF16) for s in range(2)
@@ -195,11 +226,19 @@
     place = lax.broadcasted_iota(jnp.int32, (mdev, mrows), 0) + d * mdev
     mine = jnp.where(lane == place, sections[...].astype(F32), 0.0)
     section = jnp.sum(mine, axis=1, keepdims=True)
+    ar = att.shape[1]
+
+    def pack(blocks):
+        if ar > heads * qr:
+            blocks = blocks + [jnp.zeros((ar - heads * qr, HD), F32)]
+        return jnp.concatenate(blocks, axis=0).astype(BF16)
+
     acc_c = [None] * dp
     st_c = [None] * dp
     for off in list(range(1, dp)) + [0]:
         if off:
             q_c[off].wait_recv()
+        sums = []
         for k in range(heads):
             cols = slice(k * HD, (k + 1) * HD)
             qk = qm[off, k]
@@ -207,37 +246,40 @@
             s = jnp.where(ok, nt(mem_k[:, cols], qk) * INV, MASKED)
             top = jnp.max(s, axis=0, keepdims=True)
             p = jnp.where(ok, jnp.exp(s - top), 0.0)
-            acc_s[off, k] = tn(p.astype(BF16), mem_v[:, cols]).astype(BF16)
+            sums.append(tn(p.astype(BF16), mem_v[:, cols])[:qr])
             st_s[off, 2 * k : 2 * k + 1, 0:qp] = top
             st_s[off, 2 * k + 1 : 2 * k + 2, 0:qp] = jnp.sum(p, axis=0, keepdims=True)
+        acc_s[off] = pack(sums)
         if off:
             st_c[off] = send(st_s.at[off], st_r.at[off], st_ss.at[off], st_rs.at[off], at_dp(-off))
             acc_c[off] = send(
                 acc_s.at[off], acc_r.at[off], acc_ss.at[off], acc_rs.at[off], at_dp(-off)
             )
 
+    def merge(state, offs):
+        stats = [jnp.transpose((st_r if off else st_s)[off]) for off in offs]
+        terms = [(acc_r if off else acc_s)[off].astype(F32) for off in offs]
+        merged = []
+        for k in range(heads):
+            top_c, total_c, acc = state[k]
+            tops = [st[:qr, 2 * k : 2 * k + 1] for st in stats]
+            top = functools.reduce(jnp.maximum, tops, top_c)
+            factor = jnp.exp(top_c - top)
+            total = total_c * factor
+            acc = acc * factor
+            for i in range(len(offs)):
+                factor = jnp.exp(tops[i] - top)
+                total = total + stats[i][:qr, 2 * k + 1 : 2 * k + 2] * factor
+                acc = acc + terms[i][k * qr : (k + 1) * qr] * factor
+            merged.append((top, total, acc))
+        return merged
+
+    own = merge(own, [0])
     for off in range(1, dp):
         st_c[off].wait_recv()
         acc_c[off].wait_recv()
-    stats = [jnp.transpose((st_r if off else st_s)[off]) for off in range(dp)]
-    blocks = []
-    for k in range(heads):
-        top_c, total_c, acc = own[k]
-        tops = [st[:qr, 2 * k : 2 * k + 1] for st in stats]
-        totals = [st[:qr, 2 * k + 1 : 2 * k + 2] for st in stats]
-        top = functools.reduce(jnp.maximum, tops, top_c)
-        factor = jnp.exp(top_c - top)
-        total = total_c * factor
-        acc = acc * factor
-        for off in range(dp):
-            factor = jnp.exp(tops[off] - top)
-            total = total + totals[off] * factor
-            acc = acc + (acc_r if off else acc_s)[off, k][:qr].astype(F32) * factor
-        blocks.append(acc / total)
-    ar = att.shape[1]
-    if ar > heads * qr:
-        blocks.append(jnp.zeros((ar - heads * qr, HD), F32))
-    att[0] = jnp.concatenate(blocks, axis=0).astype(BF16)
+    own = merge(own, list(range(1, dp)))
+    att[0] = pack([acc / total for _, total, acc in own])
     att_c = [None] * dp
     for off in range(1, dp):
         att_c[off] = send(att.at[0], att.at[off], att_ss.at[off], att_rs.at[off], at_dp(off))
@@ -252,21 +294,29 @@
             jnp.concatenate([a[h * rows : (h + 1) * rows] for h in range(heads * PER)], axis=1)
         )
     lhs = jnp.concatenate(groups, axis=0).astype(BF16)
-    orows = osum_s.shape[1]
+    orows, ocols = osum.shape[1:]
+    cuts = osum_s.shape[1] // orows
+    span = ocols // cuts
     result = nn(lhs, wo[...])
     for i in range(tp):
-        osum_s[i] = result[i * orows : (i + 1) * orows]
+        mine = result[i * orows : (i + 1) * orows]
+        osum[i] = mine
+        osum_s[i] = jnp.concatenate(
+            [mine[:, c * span : (c + 1) * span] for c in range(cuts)], axis=0
+        ).astype(BF16)
     o_c = [None] * tp
     for off in range(1, tp):
         to = lax.rem(t + off, tp)
         o_c[off] = send(osum_s.at[to], osum_r.at[off], o_ss.at[off], o_rs.at[off], at_tp(off))
-    summed = osum_s[t]
+    own_sum = osum[t]
+    summed = [own_sum[:, c * span : (c + 1) * span] for c in range(cuts)]
     for off in range(1, tp):
         o_c[off].wait_recv()
-        summed = summed + osum_r[off]
-    out[...] = summed.astype(BF16)
-
-    for copies in (hid_c, q_c, st_c, acc_c, att_c, o_c):
+        came = osum_r[off].astype(F32)
+        summed = [v + came[c * orows : (c + 1) * orows] for c, v in enumerate(summed)]
+    out[...] = jnp.concatenate(summed, axis=1).astype(BF16)
+
+    for copies in hid_c + [q_c, st_c, acc_c, att_c, o_c]:
         for copy in copies:
             if copy is not None:
                 copy.wait_send()
@@ -295,6 +345,8 @@
     ar = up(heads * PER * rows, 16)
     ocols = out_weight.shape[1]
     orows = dp * rows // tp
+    chunks = feat // 256 if feat % 256 == 0 else 1
+    cuts = ocols // HD if ocols % HD == 0 else 1
     any_spec = pl.BlockSpec(memory_space=pl.ANY)
     smem = pl.BlockSpec(memory_space=pltpu.SMEM)
     dma = pltpu.SemaphoreType.DMA
@@ -306,7 +358,7 @@
         in_specs=[smem, smem] + [any_spec] * 10,
         out_specs=pl.BlockSpec(memory_space=pltpu.VMEM),
         scratch_shapes=[
-            pltpu.VMEM((tp, mdev, feat), BF16),
+            pltpu.VMEM((tp, chunks, mdev, feat // chunks), BF16),
             like(kv_weight),
             like(kv_bias),
             like(sections),
@@ -317,16 +369,17 @@
             like(cache_values),
             like(out_weight),
             pltpu.VMEM((dp, heads, qp, HD), BF16),
-            pltpu.VMEM((dp, heads, qp, HD), BF16),
-            pltpu.VMEM((dp, heads, qp, HD), BF16),
+            pltpu.VMEM((dp, ar, HD), BF16),
+            pltpu.VMEM((dp, ar, HD), BF16),
             pltpu.VMEM((dp, 8, HD), F32),
             pltpu.VMEM((dp, 8, HD), F32),
             pltpu.VMEM((dp, ar, HD), BF16),
             pltpu.VMEM((tp, orows, ocols), F32),
-            pltpu.VMEM((tp, orows, ocols), F32),
-            dma((10,)),
-            dma((tp,)),
-            dma((tp,)),
+            pltpu.VMEM((tp, orows * cuts, ocols // cuts), BF16),
+            pltpu.VMEM((tp, orows * cuts, ocols // cuts), BF16),
+            dma((9 + chunks,)),
+            dma((tp, chunks)),
+            dma((tp, chunks)),
         ]
         + [dma((dp,))] * 8
         + [dma((tp,))] * 2,

time: 28.2 us -> 27.9 us (0.989)
  no operation moved by 1% of the time
where the time goes in v3:
time: 27.9 us; the launch traced here: 27.7 us
  Pallas kernels  25.8 us (92%)
  local copies, waits for them, and re-layouts  1.34 us (5%)
  between operations  0.66 us (2%)
    pallas_call x1, Pallas kernels, body(): pl.pallas_call(functools.partial(kernel, tp, dp), out_shape=jax.ShapeDtyp...  25.8 us
    unnamed x1, local copies, waits for them, and re-layouts  1.34 us

profile of v3, /device:TPU:0, one launch (start us, length us, event | category | flops | bytes accessed | tf_op | source)
XLA Modules:
  0.0 27.7 jit_solution(16258418623537427836)
XLA Ops:
  0.7 25.8 %decode_step.1 = bf16[8,1280]{1,0:T(8,128)(2,1)} custom-call(s32[4]{0:T(128)} %lens.1, s32[1]{0:T(128)S(6)} %copy.14.group, bf16[64,1280]{1,0:T(8,128)(2,1)} %hidden_h.1, bf16[2,5120,256]{2,1,0:T(8,128)(2,1)} %kvw_h.1, bf16[2,256]{1,0:T(2,128)(2,1)} %bias_h.1, s32[1,256]{1,0:T(1,128)} %bitcast.1, bf16[8,1280]{1,0:T(8,128)(2,1)} %q_h.1, bf16[8,256]{1,0:T(8,128)(2,1)} %nk_h.1, ...), custom_call_target="tpu_custom_call" | custom-call | tf_op jit(solution)/shard_map/decode_step/pallas_call | solution.py:355
  26.4 1.3 %copy.15 = bf16[8,1280]{1,0:T(8,128)(2,1)} copy(bf16[8,1280]{1,0:T(8,128)(2,1)} %decode_step.1) | data formatting | bytes 40960

commit v4 on v3

--- a/solution.py
+++ b/solution.py
@@ -102,6 +102,12 @@
     def at_dp(off):
         return {"dp": lax.rem(d + off + dp, dp)}
 
+    barrier = pltpu.get_barrier_semaphore()
+    for off in range(1, tp):
+        pl.semaphore_signal(barrier, inc=1, device_id=at_tp(off), device_id_type=MESH)
+    for off in range(1, dp):
+        pl.semaphore_signal(barrier, inc=1, device_id=at_dp(off), device_id_type=MESH)
+
     pairs = (
         (q_h, q_v),
         (nk_h, nk),
@@ -116,16 +122,12 @@
         (hidden_h.at[:, c * width : (c + 1) * width], hid.at[0, c]) for c in range(chunks)
     )
     loads = [pltpu.make_async_copy(s, v, load_sem.at[i]) for i, (s, v) in enumerate(pairs)]
-    for copy in loads:
+    l_q, l_nk, l_nv, l_bias, l_sec, l_ck, l_cv, l_kvw, l_wo = loads[:9]
+
+    for copy in [l_q] + loads[9:] + [l_nk, l_nv, l_bias, l_sec, l_ck, l_cv, l_kvw]:
         copy.start()
-    l_q, l_nk, l_nv, l_bias, l_sec, l_ck, l_cv, l_kvw, l_wo = loads[:9]
-
-    barrier = pltpu.get_barrier_semaphore()
-    for off in range(1, tp):
-        pl.semaphore_signal(barrier, inc=1, device_id=at_tp(off), device_id_type=MESH)
-    for off in range(1, dp):
-        pl.semaphore_signal(barrier, inc=1, device_id=at_dp(off), device_id_type=MESH)
-
+    for copy in loads[9:]:
+        copy.wait()
     pl.semaphore_wait(barrier, tp - 1 + dp - 1)
 
     def send(src, dst, ss, rs, to):
@@ -155,7 +157,9 @@
 
     for slot, to in direct.items():
         for c in range(chunks):
-            send_hidden(slot, c, hidden_h.at[:, c * width : (c + 1) * width], to)
+            send_hidden(slot, c, hid.at[0, c], to)
+
+    l_wo.start()
 
     l_q.wait()
     q_wide = q_v[...].astype(F32)
@@ -200,8 +204,6 @@
     l_kvw.wait()
     proj = [jnp.zeros((mdev, heads * HD), F32) for _ in range(2)]
     squares = jnp.zeros((mdev, 1), F32)
-    for copy in loads[9:]:
-        copy.wait()
     handed = min(heads, chunks)
     for slot in range(tp):
         if relay and slot == 2:
@@ -345,7 +347,7 @@
     ar = up(heads * PER * rows, 16)
     ocols = out_weight.shape[1]
     orows = dp * rows // tp
-    chunks = feat // 256 if feat % 256 == 0 else 1
+    chunks = feat // 640 if feat % 640 == 0 else 1
     cuts = ocols // HD if ocols % HD == 0 else 1
     any_spec = pl.BlockSpec(memory_space=pl.ANY)
     smem = pl.BlockSpec(memory_space=pltpu.SMEM)

time: 27.9 us -> 27.5 us (0.986)
  Pallas kernels: 25.8 us -> 25.3 us
    pallas_call x1, Pallas kernels: 25.8 us -> 25.3 us  [body(): pl.pallas_call(functools.partial(kernel, tp, dp), out_shape=jax.ShapeDtyp...]
where the time goes in v4:
time: 27.5 us; the launch traced here: 27.3 us
  Pallas kernels  25.3 us (92%)
  local copies, waits for them, and re-layouts  1.34 us (5%)
  between operations  0.66 us (2%)
    pallas_call x1, Pallas kernels, body(): pl.pallas_call(functools.partial(kernel, tp, dp), out_shape=jax.ShapeDtyp...  25.3 us
    unnamed x1, local copies, waits for them, and re-layouts  1.34 us

profile of v4, /device:TPU:0, one launch (start us, length us, event | category | flops | bytes accessed | tf_op | source)
XLA Modules:
  0.0 27.3 jit_solution(3570857198868905594)
XLA Ops:
  0.7 25.3 %decode_step.1 = bf16[8,1280]{1,0:T(8,128)(2,1)} custom-call(s32[4]{0:T(128)} %lens.1, s32[1]{0:T(128)S(6)} %copy.14.group, bf16[64,1280]{1,0:T(8,128)(2,1)} %hidden_h.1, bf16[2,5120,256]{2,1,0:T(8,128)(2,1)} %kvw_h.1, bf16[2,256]{1,0:T(2,128)(2,1)} %bias_h.1, s32[1,256]{1,0:T(1,128)} %bitcast.1, bf16[8,1280]{1,0:T(8,128)(2,1)} %q_h.1, bf16[8,256]{1,0:T(8,128)(2,1)} %nk_h.1, ...), custom_call_target="tpu_custom_call" | custom-call | tf_op jit(solution)/shard_map/decode_step/pallas_call | solution.py:357
  26.0 1.3 %copy.15 = bf16[8,1280]{1,0:T(8,128)(2,1)} copy(bf16[8,1280]{1,0:T(8,128)(2,1)} %decode_step.1) | data formatting | bytes 40960
